TPU v7x, 32 devices: a whole 2x2x4 slice. The times are simulated.
32 devices in a mesh: grp: 8 (over z, y), band: 4 (over x, core).
Axes of the slice: x: 2, y: 2, z: 4, core: 2. Of those that a mesh axis runs over, the one named last changes fastest.
Arguments:
- spectra: bfloat16 [2, 32, 32, 1024], P(None, None, 'band', 'grp'), may hold values from -140 to 140, as said below
- tile_band: int32 [8, 8], P('grp'), may hold values from 0 to 4, as said below
Outputs:
- gathers: bfloat16 [8, 4, 32, 128, 256], P('grp', 'band')
Inputs may be any that keep to these rules, and one draw needn't show every extreme that they name: `spectra`: entries are of order one times a scale of each window and channel. `tile_band`: entry (i, j) is |i - j| * 4 // 8, or 4 where the pair is not stacked; it is 4 where i = j, and never 4 where |i - j| = 1.
All inputs are finite; a program needn't handle non-finite values.
Results may differ from a plain program's by a relative error of at most 0.0064.
Values may be sent and summed in bfloat16 or wider, within the bound.
A program may use at most 64 MiB of HBM per device.

v0:
```python
import jax
import jax.numpy as jnp
from jax import lax
from jax.sharding import PartitionSpec as P

BAND_DEV = 1


def stack_of(own, partner, weights, sources, tile):
    windows = own.shape[1]
    bin_count = own.shape[2]
    own_view = own.reshape(2, windows, bin_count, sources, tile)
    real_part = partner[:, :, 0]
    imag_part = partner[:, :, 1]
    paired = jnp.stack(
        [jnp.stack([real_part, imag_part], axis=4), jnp.stack([imag_part, -real_part], axis=4)],
        axis=2,
    )
    gram = jnp.einsum("pwfsa,skpwfqb->skfaqb", own_view, paired, preferred_element_type=jnp.float32)
    gram = gram.reshape(sources, partner.shape[1], bin_count, tile, 2 * tile)
    return (gram / jnp.maximum(weights, 1.0)[:, :, None, None, None]).astype(jnp.bfloat16)


def local(spectra, tile_band):
    windows = spectra.shape[1]
    bin_count = spectra.shape[2]
    sources = tile_band.shape[0]
    tile = spectra.shape[3] // sources
    bands = BAND_DEV * lax.axis_size("band")
    values = spectra.astype(jnp.float32)
    power = jnp.sum(values * values, axis=(0, 2))
    power = lax.psum(power, "band")
    factor = lax.rsqrt(power / (bin_count * lax.axis_size("band")) + 1e-05)
    white = (values * factor[None, :, None, :]).astype(jnp.bfloat16)
    selector = (tile_band[:, None, :] == jnp.arange(bands, dtype=jnp.int32)[None, :, None]).astype(
        jnp.bfloat16
    )
    counts = jnp.sum(selector.astype(jnp.float32), axis=2)
    piece = lax.all_gather(white, "grp", axis=3, tiled=True)
    span = piece.shape[3] // tile
    piece_view = piece.reshape(2, windows, bin_count, span, tile)
    summed = jnp.einsum(
        "skn,pwfnc->skpwfc", selector, piece_view, preferred_element_type=jnp.float32
    ).astype(jnp.bfloat16)
    moved = lax.all_to_all(summed, "band", split_axis=1, concat_axis=4, tiled=True)
    whole = lax.all_gather(white, "band", axis=2, tiled=True)
    mine = lax.dynamic_slice_in_dim(counts, lax.axis_index("band") * BAND_DEV, BAND_DEV, 1)
    return stack_of(whole, moved, mine, sources, tile)


def solution(mesh):
    return jax.shard_map(
        local,
        mesh=mesh,
        in_specs=(P(None, None, "band", "grp"), P("grp", None)),
        out_specs=P("grp", "band", None, None, None),
        check_vma=False,
    )
```

profile of v0, /device:TPU:0, one launch (start us, length us, event | category | flops | bytes accessed | tf_op | source)
XLA Modules:
  0.0 91.7 jit_solution(2831564745839331442)
XLA Ops:
  6.5 0.0 copy-start.1
  6.5 0.0 all-gather.2.cloned.1.call-start
  6.5 0.9 %fusion.6 = f32[32,128]{1,0:T(8,128)S(1)} fusion(bf16[2,32,8,128]{3,2,1,0:T(8,128)(2,1)} %param.2), kind=kLoop, calls=%fused_computation.14 | loop fusion | flops 192512 | bytes 147456 | tf_op jit(solution)/shard_map/reduce_sum | solution.py:31
  7.5 12.7 %psum.7 = f32[32,128]{1,0:T(8,128)S(1)} all-reduce(f32[32,128]{1,0:T(8,128)S(1)} %fusion.6), channel_id=1, replica_groups=mesh['grp'=8,'band'=4] {'band'}, use_global_device_ids=true, to_apply=%region_1.0 | all-reduce | flops 4096 | bytes 32768 | tf_op jit(solution)/shard_map/psum | solution.py:32
  20.2 1.6 %fusion.7 = bf16[2,32,8,128]{3,1,0,2:T(8,128)(2,1)} fusion(f32[32,128]{1,0:T(8,128)S(1)} %add_rsqrt_fusion, bf16[2,32,8,128]{3,2,1,0:T(8,128)(2,1)} %param.2), kind=kLoop, calls=%fused_computation.15 | loop fusion | flops 196608 | bytes 278528 | tf_op jit(solution)/shard_map/convert_element_type | solution.py:34
  21.7 0.0 all-gather.2.cloned.1.call-update
  21.8 40.0 %all-gather.2.cloned.1.call-done = bf16[2,32,8,1024]{3,1,0,2:T(8,128)(2,1)} async-done(((bf16[2,32,8,128]{3,1,0,2:T(8,128)(2,1)}), bf16[2,32,8,1024]{3,1,0,2:T(8,128)(2,1)}) %all-gather.2.cloned.1.call-update) | async-done | bytes 1048592 | tf_op jit(solution)/shard_map/all_gather | solution.py:39
  61.8 1.5 %copy.36 = bf16[64,8,8,128]{3,2,1,0:T(8,128)(2,1)S(1)} copy(bf16[64,8,8,128]{3,1,2,0:T(8,128)(2,1)} %bitcast.56) | data formatting | bytes 2097152
  63.3 0.0 copy-start
  63.3 0.0 copy-done.1
  63.3 0.4 fusion.1
  63.7 0.9 copy.24
  64.6 3.5 %all-to-all-start = ((bf16[1,4,2,32,8,128]{5,4,3,2,0,1:T(8,128)(2,1)}), bf16[1,4,2,32,8,128]{5,4,3,2,0,1:T(8,128)(2,1)S(1)}, u32[]{:S(2)}, u32[]{:S(2)}) async-start(bf16[1,4,2,32,8,128]{5,4,3,2,0,1:T(8,128)(2,1)} %copy.24), calls=%async_computation | async-start | bytes 1048576 | tf_op jit(solution)/shard_map/all_to_all | solution.py:45
  68.1 0.1 convert_reduce_fusion
  68.2 0.6 dynamic-slice.3
  69.5 0.0 copy-done
  69.5 11.1 %all_gather.7 = bf16[2,32,32,128]{3,1,0,2:T(8,128)(2,1)S(1)} all-gather(bf16[2,32,8,128]{3,1,0,2:T(8,128)(2,1)S(1)} %copy-done), channel_id=1, replica_groups=mesh['grp'=8,'band'=4] {'band'}, dimensions={2}, use_global_device_ids=true | all-gather | bytes 655360 | tf_op jit(solution)/shard_map/all_gather | solution.py:46
  80.6 0.0 all-to-all-done
  80.6 0.1 copy.46
  80.7 0.1 fusion.13
  80.8 0.2 copy_bitcast_fusion.1
  81.0 0.1 maximum_bitcast_fusion.2
  81.1 0.8 fusion
  82.0 2.9 %copy.29 = bf16[1,1,32,128,256]{4,3,2,1,0:T(8,128)(2,1)} copy(bf16[1,1,32,128,256]{3,4,2,1,0:T(8,128)(2,1)S(1)} %bitcast.54) | data formatting | bytes 4194304 | tf_op jit(solution)/shard_map/convert_element_type | solution.py:21
  (2 shorter events, 0.0 us)
Async XLA Ops:
  6.5 56.7 %copy-start.1 = (s32[1,8]{1,0:T(1,128)S(1)}, s32[1,8]{1,0:T(1,128)}, u32[]{:S(2)}) copy-start(s32[1,8]{1,0:T(1,128)} %param.3) | copy-start | bytes 100
  6.5 55.2 %all-gather.2.cloned.1.call-start = ((), (), s32[]{:S(2)}) async-start(), calls=%async_computation.1 | async-start | bytes 1179648 | tf_op jit(solution)/shard_map/all_gather | solution.py:39
  63.3 6.2 %copy-start = (bf16[2,32,8,128]{3,1,0,2:T(8,128)(2,1)S(1)}, bf16[2,32,8,128]{3,1,0,2:T(8,128)(2,1)}, u32[]{:S(2)}) copy-start(bf16[2,32,8,128]{3,1,0,2:T(8,128)(2,1)} %fusion.7) | copy-start | bytes 393220
  64.6 16.0 %all-to-all-start = ((bf16[1,4,2,32,8,128]{5,4,3,2,0,1:T(8,128)(2,1)}), bf16[1,4,2,32,8,128]{5,4,3,2,0,1:T(8,128)(2,1)S(1)}, u32[]{:S(2)}, u32[]{:S(2)}) async-start(bf16[1,4,2,32,8,128]{5,4,3,2,0,1:T(8,128)(2,1)} %copy.24), calls=%async_computation | async-start | bytes 1048576 | tf_op jit(solution)/shard_map/all_to_all | solution.py:45
Sparse Core Ops, SparseCore 0:
  21.9 39.8 all-gather.1
where the time goes:
time: 92 us; the launch traced here: 91.7 us
  waiting for transfers between devices  40 us (43%)
  blocking collectives  23.7 us (26%)
  between operations  14.1 us (15%)
  local copies, waits for them, and re-layouts  6.22 us (7%)
  starting transfers between devices  3.47 us (4%)
  other arithmetic  2.85 us (3%)
  matrix products  1.26 us (1%)
    all_gather x1, waiting for transfers between devices, local(): piece = lax.all_gather(white, 'grp', axis=3, tiled=True)  40 us
    psum x1, blocking collectives, local(): power = lax.psum(power, 'band')  12.7 us
    all_gather x1, blocking collectives, local(): whole = lax.all_gather(white, 'band', axis=2, tiled=True)  11.1 us
    all_to_all x1, starting transfers between devices, local(): lax.all_to_all(summed, 'band', split_axis=1, concat_axis=4, tiled=True)  3.47 us
    convert_element_type x1, local copies, waits for them, and re-layouts, stack_of(): (gram / jnp.maximum(weights, 1.0)[:, :, None, None, None]).astype(jnp.bfl...  2.89 us
  transfers between devices with their start and end apart: 2, of which 1 were waited for; matrix products, arithmetic and copies ran while one was open for 1% of the time, Pallas kernels for 0%

commit v1 on v0

v1 whole, which is shorter than its diff:
```python
import functools

import jax
import jax.numpy as jnp
from jax import lax
from jax.experimental import pallas as pl
from jax.experimental.pallas import tpu as pltpu
from jax.sharding import PartitionSpec as P

LINES = 4
CHUNKS = 4
MESH = pl.DeviceIdType.MESH


def kernel(
    groups, bands, bins, windows, chunks,
    tb_ref, x_ref, out_ref,
    raw, power, blocks, sums, own, partner,
    p_send, p_recv, line_send, side_send, block_recv, own_send, own_recv, sum_send, sum_recv,
):
    g = lax.axis_index("grp")
    b = lax.axis_index("band")
    inner = groups // LINES
    row, col = g // inner, lax.rem(g, inner)
    rows = 2 * windows
    part = bins // chunks
    half = row // 2
    near = [row + 1 - 2 * lax.rem(row, 2), 2 - half, 3 - 3 * half]
    line = [r * inner + col for r in near]
    side = [lax.rem(col + e, inner) for e in range(1, inner)]
    peer = [lax.rem(b + e, bands) for e in range(bands)]

    barrier = pltpu.get_barrier_semaphore()
    for j in line:
        pl.semaphore_signal(barrier, inc=1, device_id=(j, b), device_id_type=MESH)
    for s in side:
        pl.semaphore_signal(barrier, inc=1, device_id=(row * inner + s, b), device_id_type=MESH)
    for k in peer[1:]:
        pl.semaphore_signal(barrier, inc=1, device_id=(g, k), device_id_type=MESH)

    raw[...] = x_ref[...].astype(jnp.float32)
    total = jnp.zeros((rows, raw.shape[1]), jnp.float32)
    for f in range(bins):
        v = raw[pl.ds(f, rows, stride=bins), :]
        total = total + v * v
    power[b] = total[:windows] + total[windows:]

    pl.semaphore_wait(barrier, len(line) + len(side) + bands - 1)

    def power_copy(e):
        return pltpu.make_async_remote_copy(
            src_ref=power.at[b], dst_ref=power.at[b], send_sem=p_send.at[e - 1], recv_sem=p_recv.at[e - 1],
            device_id=(g, peer[e]), device_id_type=MESH,
        )

    def block_copy(j, c, send_sem, target):
        view = blocks.at[j, pl.ds(c * part, part)]
        return pltpu.make_async_remote_copy(
            src_ref=view, dst_ref=view, send_sem=send_sem, recv_sem=block_recv.at[j, c],
            device_id=(target, b), device_id_type=MESH,
        )

    def line_copy(t, c):
        return block_copy(g, c, line_send.at[t, c], line[t])

    def side_copy(e, r, slot, c):
        return block_copy(r * inner + col, c, side_send.at[e, slot, c], row * inner + side[e])

    def block_wait(j, c):
        block_copy(j, c, line_send.at[0, c], line[0]).wait_recv()

    def own_copy(e):
        return pltpu.make_async_remote_copy(
            src_ref=blocks.at[g], dst_ref=own.at[b], send_sem=own_send.at[e - 1], recv_sem=own_recv.at[e - 1],
            device_id=(g, peer[e]), device_id_type=MESH,
        )

    def sum_copy(e, c):
        return pltpu.make_async_remote_copy(
            src_ref=sums.at[e - 1, pl.ds(c * part, part)], dst_ref=partner.at[b, pl.ds(c * part, part)],
            send_sem=sum_send.at[e - 1, c], recv_sem=sum_recv.at[e - 1, c],
            device_id=(g, peer[e]), device_id_type=MESH,
        )

    for e in range(1, bands):
        power_copy(e).start()
    for e in range(1, bands):
        power_copy(e).wait_recv()
    whole = power[0]
    for e in range(1, bands):
        whole = whole + power[e]
    factor = lax.rsqrt(whole / (bins * bands) + 1e-05)
    factor = jnp.concatenate([factor, factor], axis=0)
    for c in range(chunks):
        for f in range(c * part, (c + 1) * part):
            v = (raw[pl.ds(f, rows, stride=bins), :] * factor).astype(jnp.bfloat16)
            blocks[g, f] = v
            own[b, f] = v
        for e in range(len(side)):
            side_copy(e, row, 0, c).start()
        for t in range(len(line)):
            line_copy(t, c).start()
    for e in range(1, bands):
        own_copy(e).start()

    def forward(c):
        for t in range(len(line)):
            block_wait(line[t], c)
            for e in range(len(side)):
                side_copy(e, near[t], t + 1, c).start()

    def pick(j, k):
        inside = (j >= 0) & (j < groups)
        at = jnp.clip(j, 0, groups - 1)
        return at, jnp.where(inside & (tb_ref[0, at] == k), 1.0, 0.0)

    reach = groups // bands

    def band_sum(c):
        for s in side:
            for r in [row] + near:
                block_wait(r * inner + s, c)
        for e in list(range(1, bands)) + [0]:
            k = peer[e]
            terms = []
            for q in range(reach):
                d = k * reach + q
                terms.append(pick(g + d, k))
                at, weight = pick(g - d, k)
                terms.append((at, jnp.where(d > 0, weight, 0.0)))
            for f in range(c * part, (c + 1) * part):
                acc = None
                for at, weight in terms:
                    term = blocks[at, f].astype(jnp.float32) * weight
                    acc = term if acc is None else acc + term
                acc = acc.astype(jnp.bfloat16)
                if e == 0:
                    partner[b, f] = acc
                else:
                    sums[e - 1, f] = acc
            if e > 0:
                sum_copy(e, c).start()

    count = jnp.float32(0.0)
    for j in range(groups):
        count = count + jnp.where(tb_ref[0, j] == b, 1.0, 0.0)
    scale = 1.0 / jnp.maximum(jnp.full((1, 2 * raw.shape[1]), count, jnp.float32), 1.0)

    def gram(c):
        for e in range(bands):
            if e > 0:
                if c == 0:
                    own_copy(e).wait_recv()
                sum_copy(e, c).wait_recv()
            owner = lax.rem(b + bands - e, bands)
            for f in range(c * part, (c + 1) * part):
                y = partner[owner, f]
                turned = jnp.concatenate([y[windows:], -y[:windows]], axis=0)
                both = jnp.concatenate([y, turned], axis=1)
                tile = lax.dot_general(
                    own[owner, f], both, (((0,), (0,)), ((), ())), preferred_element_type=jnp.float32
                )
                out_ref[owner * bins + f] = (tile * scale).astype(jnp.bfloat16)

    forward(0)
    for c in range(chunks):
        if c + 1 < chunks:
            forward(c + 1)
        band_sum(c)
        if c > 0:
            gram(c - 1)
    gram(chunks - 1)

    for e in range(1, bands):
        power_copy(e).wait_send()
        own_copy(e).wait_send()
    for c in range(chunks):
        for t in range(len(line)):
            line_copy(t, c).wait_send()
        for e in range(len(side)):
            for slot, r in enumerate([row] + near):
                side_copy(e, r, slot, c).wait_send()
        for e in range(1, bands):
            sum_copy(e, c).wait_send()


def local(groups, bands, spectra, tile_band):
    _, windows, bins, tile = spectra.shape
    rows = 2 * windows
    flat = spectra.reshape(rows * bins, tile)
    inner = groups // LINES
    dma = pltpu.SemaphoreType.DMA
    out = pl.pallas_call(
        functools.partial(kernel, groups, bands, bins, windows, CHUNKS),
        out_shape=jax.ShapeDtypeStruct((bands * bins, tile, 2 * tile), jnp.bfloat16),
        in_specs=[pl.BlockSpec(memory_space=pltpu.SMEM), pl.BlockSpec(memory_space=pltpu.VMEM)],
        out_specs=pl.BlockSpec(memory_space=pltpu.VMEM),
        scratch_shapes=[
            pltpu.VMEM((rows * bins, tile), jnp.float32),
            pltpu.VMEM((bands, windows, tile), jnp.float32),
            pltpu.VMEM((groups, bins, rows, tile), jnp.bfloat16),
            pltpu.VMEM((bands - 1, bins, rows, tile), jnp.bfloat16),
            pltpu.VMEM((bands, bins, rows, tile), jnp.bfloat16),
            pltpu.VMEM((bands, bins, rows, tile), jnp.bfloat16),
            dma((bands - 1,)),
            dma((bands - 1,)),
            dma((LINES - 1, CHUNKS)),
            dma((inner - 1, LINES, CHUNKS)),
            dma((groups, CHUNKS)),
            dma((bands - 1,)),
            dma((bands - 1,)),
            dma((bands - 1, CHUNKS)),
            dma((bands - 1, CHUNKS)),
        ],
        compiler_params=pltpu.CompilerParams(
            collective_id=0, has_side_effects=True, vmem_limit_bytes=32 * 1024 * 1024
        ),
    )(tile_band, flat)
    return out.reshape(1, 1, bands * bins, tile, 2 * tile)


def solution(mesh):
    return jax.shard_map(
        functools.partial(local, mesh.shape["grp"], mesh.shape["band"]),
        mesh=mesh,
        in_specs=(P(None, None, "band", "grp"), P("grp", None)),
        out_specs=P("grp", "band", None, None, None),
        check_vma=False,
    )
```

time: 92 us -> 35.1 us (0.38)
  waiting for transfers between devices: 40 us -> 0 us
  Pallas kernels: 0 us -> 32.1 us
  blocking collectives: 23.7 us -> 0 us
  between operations: 14.1 us -> 0.01 us
  starting transfers between devices: 3.47 us -> 0 us
  local copies, waits for them, and re-layouts: 6.22 us -> 2.88 us
  other arithmetic: 2.85 us -> 0 us
  matrix products: 1.26 us -> 0 us
    all_gather x1 -> x0, waiting for transfers between devices: 40 us -> none  [local(): piece = lax.all_gather(white, 'grp', axis=3, tiled=True)]
    pallas_call x0 -> x1, Pallas kernels: none -> 32.1 us  [local(): pl.pallas_call(functools.partial(kernel, groups, bands, bins, windows, CH...]
    psum x1 -> x0, blocking collectives: 12.7 us -> none  [local(): power = lax.psum(power, 'band')]
    all_gather x1 -> x0, blocking collectives: 11.1 us -> none  [local(): whole = lax.all_gather(white, 'band', axis=2, tiled=True)]
    convert_element_type x2 -> x0, local copies, waits for them, and re-layouts: 3.77 us -> none  [the longest x1 2.89 us: stack_of(): (gram / jnp.maximum(weights, 1.0)[:, :, None, None, None]).astype(jnp.bfl...]
    all_to_all x1 -> x0, starting transfers between devices: 3.47 us -> none  [local(): lax.all_to_all(summed, 'band', split_axis=1, concat_axis=4, tiled=True)]
    convert_element_type x1 -> x0, other arithmetic: 1.58 us -> none  [local(): white = (values * factor[None, :, None, :]).astype(jnp.bfloat16)]
    unnamed x5, local copies, waits for them, and re-layouts: 1.49 us -> 2.88 us
  transfers between devices with their start and end apart: 2 -> 0, of which waited for: 1 -> 0; matrix products, arithmetic and copies ran while one was open for 1% -> 0% of each run, Pallas kernels for 0% -> 0%
where the time goes in v1:
time: 35.1 us; the launch traced here: 34.9 us
  Pallas kernels  32.1 us (91%)
  local copies, waits for them, and re-layouts  2.88 us (8%)
    pallas_call x1, Pallas kernels, local(): pl.pallas_call(functools.partial(kernel, groups, bands, bins, windows, CH...  32.1 us
    unnamed x5, local copies, waits for them, and re-layouts  2.88 us

profile of v1, /device:TPU:0, one launch (start us, length us, event | category | flops | bytes accessed | tf_op | source)
XLA Modules:
  0.0 34.9 jit_solution(15477646334714295124)
XLA Ops:
  0.0 0.0 copy-start
  0.0 0.9 %copy-done = bf16[2,32,8,128]{3,2,1,0:T(8,128)(2,1)S(1)} copy-done((bf16[2,32,8,128]{3,2,1,0:T(8,128)(2,1)S(1)}, bf16[2,32,8,128]{3,2,1,0:T(8,128)(2,1)}, u32[]{:S(2)}) %copy-start) | copy-done | bytes 131096
  0.9 0.0 copy-start.1
  0.9 0.7 %copy-done.1 = s32[1,8]{1,0:T(1,128)S(1)} copy-done((s32[1,8]{1,0:T(1,128)S(1)}, s32[1,8]{1,0:T(1,128)}, u32[]{:S(2)}) %copy-start.1) | copy-done | bytes 56
  1.6 32.1 %shard_map.28 = bf16[32,128,256]{2,1,0:T(8,128)(2,1)S(1)} custom-call(s32[1,8]{1,0:T(1,128)S(1)} %copy-done.1, bf16[512,128]{1,0:T(8,128)(2,1)S(1)} %bitcast.3), custom_call_target="tpu_custom_call" | custom-call | tf_op jit(solution)/shard_map/pallas_call | solution.py:193
  33.6 1.3 %copy.4 = bf16[1,1,32,128,256]{4,3,2,1,0:T(8,128)(2,1)} copy(bf16[1,1,32,128,256]{4,3,2,1,0:T(8,128)(2,1)S(1)} %bitcast.2) | data formatting | bytes 4194304
Async XLA Ops:
  0.0 0.9 %copy-start = (bf16[2,32,8,128]{3,2,1,0:T(8,128)(2,1)S(1)}, bf16[2,32,8,128]{3,2,1,0:T(8,128)(2,1)}, u32[]{:S(2)}) copy-start(bf16[2,32,8,128]{3,2,1,0:T(8,128)(2,1)} %param.2) | copy-start | bytes 393220
  0.9 0.7 %copy-start.1 = (s32[1,8]{1,0:T(1,128)S(1)}, s32[1,8]{1,0:T(1,128)}, u32[]{:S(2)}) copy-start(s32[1,8]{1,0:T(1,128)} %tb_ref.1) | copy-start | bytes 100

commit v2 on v1

v2 whole, which is shorter than its diff:
```python
import functools

import jax
import jax.numpy as jnp
from jax import lax
from jax.experimental import pallas as pl
from jax.experimental.pallas import tpu as pltpu
from jax.sharding import PartitionSpec as P

LINES = 4
SHARES = (1, 1, 1, 1)
CHUNKS = len(SHARES)
MESH = pl.DeviceIdType.MESH


def kernel(
    groups, bands, bins, windows, chunks,
    tb_hbm, x_hbm, out_ref,
    tb_ref, x_ref, raw, power, line_raw, side_raw, line_factor, side_factor, blocks, sums, own, partner,
    in_sem, p_send, p_recv, line_send, line_recv, first_send, first_recv, side_send, block_recv,
    lf_send, lf_recv, sf_send, sf_recv, own_send, own_recv, sum_send, sum_recv,
):
    g = lax.axis_index("grp")
    b = lax.axis_index("band")
    inner = groups // LINES
    row, col = g // inner, lax.rem(g, inner)
    rows = 2 * windows
    unit = bins // sum(SHARES)
    sizes = [n * unit for n in SHARES]
    starts = [sum(sizes[:c]) for c in range(chunks)]
    half = row // 2
    others = [row + 1 - 2 * lax.rem(row, 2), 2 - half, 3 - 3 * half]
    side = [lax.rem(col + e, inner) for e in range(1, inner)]
    source = [lax.rem(col + inner - e, inner) for e in range(1, inner)]
    peer = [lax.rem(b + e, bands) for e in range(bands)]

    barrier = pltpu.get_barrier_semaphore()
    for r in others:
        pl.semaphore_signal(barrier, inc=1, device_id=(r * inner + col, b), device_id_type=MESH)
    for s in side:
        pl.semaphore_signal(barrier, inc=1, device_id=(row * inner + s, b), device_id_type=MESH)
    for k in peer[1:]:
        pl.semaphore_signal(barrier, inc=1, device_id=(g, k), device_id_type=MESH)

    load_x = pltpu.make_async_copy(x_hbm, x_ref, in_sem.at[0])
    load_tb = pltpu.make_async_copy(tb_hbm, tb_ref, in_sem.at[1])
    load_x.start()
    load_tb.start()
    load_x.wait()
    raw[...] = x_ref[...].astype(jnp.float32)
    total = jnp.zeros((rows, raw.shape[1]), jnp.float32)
    for f in range(bins):
        v = raw[pl.ds(f, rows, stride=bins), :]
        line_raw[row, f] = v.astype(jnp.bfloat16)
        total = total + v * v
    power[b] = total[:windows] + total[windows:]
    load_tb.wait()

    pl.semaphore_wait(barrier, len(others) + len(side) + bands - 1)

    def remote(src, dst, send_sem, recv_sem, target):
        return pltpu.make_async_remote_copy(
            src_ref=src, dst_ref=dst, send_sem=send_sem, recv_sem=recv_sem,
            device_id=target, device_id_type=MESH,
        )

    def power_copy(e):
        return remote(power.at[b], power.at[b], p_send.at[e - 1], p_recv.at[e - 1], (g, peer[e]))

    def line_copy(r, c, send_sem, to):
        view = line_raw.at[r, pl.ds(starts[c], sizes[c])]
        return remote(view, view, send_sem, line_recv.at[r, c], (to * inner + col, b))

    def own_line_copy(t, c):
        return line_copy(row, c, line_send.at[t, c], others[t])

    def first_copy(e, c):
        return remote(
            line_raw.at[row, pl.ds(starts[c], sizes[c])], side_raw.at[e, pl.ds(starts[c], sizes[c])],
            first_send.at[e, c], first_recv.at[e, c], (row * inner + side[e], b),
        )

    def side_copy(e, r, c):
        j = r * inner + col
        view = blocks.at[j, pl.ds(starts[c], sizes[c])]
        return remote(view, view, side_send.at[e, r, c], block_recv.at[j, c], (row * inner + side[e], b))

    def block_wait(j, c):
        view = blocks.at[j, pl.ds(starts[c], sizes[c])]
        remote(view, view, side_send.at[0, 0, c], block_recv.at[j, c], (g, peer[1])).wait_recv()

    def line_factor_copy(t):
        view = line_factor.at[row]
        return remote(view, view, lf_send.at[t], lf_recv.at[row], (others[t] * inner + col, b))

    def side_factor_copy(e):
        return remote(
            line_factor.at[row], side_factor.at[e], sf_send.at[e], sf_recv.at[e], (row * inner + side[e], b)
        )

    def own_copy(e):
        return remote(blocks.at[g], own.at[b], own_send.at[e - 1], own_recv.at[e - 1], (g, peer[e]))

    def sum_copy(e, c):
        span = pl.ds(starts[c], sizes[c])
        return remote(
            sums.at[e - 1, span], partner.at[b, span], sum_send.at[e - 1, c], sum_recv.at[e - 1, c], (g, peer[e])
        )

    def whiten(value, factor):
        both = jnp.concatenate([factor, factor], axis=0)
        return (value.astype(jnp.float32) * both).astype(jnp.bfloat16)

    for e in range(1, bands):
        power_copy(e).start()
    for c in range(chunks):
        for e in range(len(side)):
            first_copy(e, c).start()
        if c == 0:
            for t in range(len(others)):
                own_line_copy(t, c).start()

    for e in range(1, bands):
        power_copy(e).wait_recv()
    whole = power[0]
    for e in range(1, bands):
        whole = whole + power[e]
    factor = lax.rsqrt(whole / (bins * bands) + 1e-05)
    line_factor[row] = factor
    for t in range(len(others)):
        line_factor_copy(t).start()
    for e in range(len(side)):
        side_factor_copy(e).start()
    for c in range(1, chunks):
        for t in range(len(others)):
            own_line_copy(t, c).start()
    for f in range(bins):
        v = whiten(line_raw[row, f], factor)
        blocks[g, f] = v
        own[b, f] = v
    for e in range(1, bands):
        own_copy(e).start()
    def arrive(r, c):
        j = r * inner + col
        for f in range(starts[c], starts[c] + sizes[c]):
            blocks[j, f] = whiten(line_raw[r, f], line_factor[r])
        for e in range(len(side)):
            side_copy(e, r, c).start()

    def forward(c):
        for r in others:
            if c == 0:
                view = line_factor.at[r]
                remote(view, view, lf_send.at[0], lf_recv.at[r], (g, peer[1])).wait_recv()
            line_copy(r, c, line_send.at[0, c], others[0]).wait_recv()
            arrive(r, c)

    def pick(j, k):
        inside = (j >= 0) & (j < groups)
        at = jnp.clip(j, 0, groups - 1)
        return at, jnp.where(inside & (tb_ref[0, at] == k), 1.0, 0.0)

    reach = groups // bands

    def band_sum(c):
        for e in range(len(side)):
            if c == 0:
                side_factor_copy(e).wait_recv()
            first_copy(e, c).wait_recv()
            for f in range(starts[c], starts[c] + sizes[c]):
                blocks[row * inner + source[e], f] = whiten(side_raw[e, f], side_factor[e])
            for r in others:
                block_wait(r * inner + source[e], c)
        for e in list(range(1, bands)) + [0]:
            k = peer[e]
            terms = []
            for q in range(reach):
                d = k * reach + q
                terms.append(pick(g + d, k))
                at, weight = pick(g - d, k)
                terms.append((at, jnp.where(d > 0, weight, 0.0)))
            for f in range(starts[c], starts[c] + sizes[c]):
                acc = None
                for at, weight in terms:
                    term = blocks[at, f].astype(jnp.float32) * weight
                    acc = term if acc is None else acc + term
                acc = acc.astype(jnp.bfloat16)
                if e == 0:
                    partner[b, f] = acc
                else:
                    sums[e - 1, f] = acc
            if e > 0:
                sum_copy(e, c).start()

    count = jnp.float32(0.0)
    for j in range(groups):
        count = count + jnp.where(tb_ref[0, j] == b, 1.0, 0.0)
    scale = 1.0 / jnp.maximum(jnp.full((1, 2 * raw.shape[1]), count, jnp.float32), 1.0)

    def gram(c):
        for e in range(bands):
            if e > 0:
                if c == 0:
                    own_copy(e).wait_recv()
                sum_copy(e, c).wait_recv()
            owner = lax.rem(b + bands - e, bands)
            for f in range(starts[c], starts[c] + sizes[c]):
                y = partner[owner, f]
                turned = jnp.concatenate([y[windows:], -y[:windows]], axis=0)
                both = jnp.concatenate([y, turned], axis=1)
                tile = lax.dot_general(
                    own[owner, f], both, (((0,), (0,)), ((), ())), preferred_element_type=jnp.float32
                )
                out_ref[owner * bins + f] = (tile * scale).astype(jnp.bfloat16)

    forward(0)
    for c in range(chunks):
        if c + 1 < chunks:
            forward(c + 1)
        band_sum(c)
        if c > 0:
            gram(c - 1)
    gram(chunks - 1)

    for e in range(1, bands):
        power_copy(e).wait_send()
        own_copy(e).wait_send()
    for t in range(len(others)):
        line_factor_copy(t).wait_send()
    for e in range(len(side)):
        side_factor_copy(e).wait_send()
    for c in range(chunks):
        for e in range(len(side)):
            first_copy(e, c).wait_send()
            for r in others:
                side_copy(e, r, c).wait_send()
        for e in range(1, bands):
            sum_copy(e, c).wait_send()
        for t in range(len(others)):
            own_line_copy(t, c).wait_send()


def local(groups, bands, spectra, tile_band):
    _, windows, bins, tile = spectra.shape
    rows = 2 * windows
    flat = spectra.reshape(rows * bins, tile)
    inner = groups // LINES
    dma = pltpu.SemaphoreType.DMA
    out = pl.pallas_call(
        functools.partial(kernel, groups, bands, bins, windows, CHUNKS),
        out_shape=jax.ShapeDtypeStruct((bands * bins, tile, 2 * tile), jnp.bfloat16),
        in_specs=[pl.BlockSpec(memory_space=pltpu.HBM)] * 2,
        out_specs=pl.BlockSpec(memory_space=pltpu.VMEM),
        scratch_shapes=[
            pltpu.SMEM((1, groups), jnp.int32),
            pltpu.VMEM((rows * bins, tile), jnp.bfloat16),
            pltpu.VMEM((rows * bins, tile), jnp.float32),
            pltpu.VMEM((bands, windows, tile), jnp.float32),
            pltpu.VMEM((LINES, bins, rows, tile), jnp.bfloat16),
            pltpu.VMEM((inner - 1, bins, rows, tile), jnp.bfloat16),
            pltpu.VMEM((LINES, windows, tile), jnp.float32),
            pltpu.VMEM((inner - 1, windows, tile), jnp.float32),
            pltpu.VMEM((groups, bins, rows, tile), jnp.bfloat16),
            pltpu.VMEM((bands - 1, bins, rows, tile), jnp.bfloat16),
            pltpu.VMEM((bands, bins, rows, tile), jnp.bfloat16),
            pltpu.VMEM((bands, bins, rows, tile), jnp.bfloat16),
            dma((2,)),
            dma((bands - 1,)),
            dma((bands - 1,)),
            dma((LINES - 1, CHUNKS)),
            dma((LINES, CHUNKS)),
            dma((inner - 1, CHUNKS)),
            dma((inner - 1, CHUNKS)),
            dma((inner - 1, LINES, CHUNKS)),
            dma((groups, CHUNKS)),
            dma((LINES - 1,)),
            dma((LINES,)),
            dma((inner - 1,)),
            dma((inner - 1,)),
            dma((bands - 1,)),
            dma((bands - 1,)),
            dma((bands - 1, CHUNKS)),
            dma((bands - 1, CHUNKS)),
        ],
        compiler_params=pltpu.CompilerParams(
            collective_id=0, has_side_effects=True, vmem_limit_bytes=32 * 1024 * 1024
        ),
    )(tile_band, flat)
    return out.reshape(1, 1, bands * bins, tile, 2 * tile)


def solution(mesh):
    return jax.shard_map(
        functools.partial(local, mesh.shape["grp"], mesh.shape["band"]),
        mesh=mesh,
        in_specs=(P(None, None, "band", "grp"), P("grp", None)),
        out_specs=P("grp", "band", None, None, None),
        check_vma=False,
    )
```

time: 35.1 us -> 31.8 us (0.906)
  Pallas kernels: 32.1 us -> 28.8 us
    pallas_call x1, Pallas kernels: 32.1 us -> 28.8 us  [local(): pl.pallas_call(functools.partial(kernel, groups, bands, bins, windows, CH...]
where the time goes in v2:
time: 31.8 us; the launch traced here: 31.7 us
  Pallas kernels  28.8 us (91%)
  local copies, waits for them, and re-layouts  2.88 us (9%)
    pallas_call x1, Pallas kernels, local(): pl.pallas_call(functools.partial(kernel, groups, bands, bins, windows, CH...  28.8 us
    unnamed x5, local copies, waits for them, and re-layouts  2.88 us

profile of v2, /device:TPU:0, one launch (start us, length us, event | category | flops | bytes accessed | tf_op | source)
XLA Modules:
  0.0 31.7 jit_solution(8035944700716830943)
XLA Ops:
  0.0 0.0 copy-start
  0.0 0.9 %copy-done = bf16[2,32,8,128]{3,2,1,0:T(8,128)(2,1)S(1)} copy-done((bf16[2,32,8,128]{3,2,1,0:T(8,128)(2,1)S(1)}, bf16[2,32,8,128]{3,2,1,0:T(8,128)(2,1)}, u32[]{:S(2)}) %copy-start) | copy-done | bytes 131096
  0.9 0.0 copy-start.1
  0.9 0.7 %copy-done.1 = s32[1,8]{1,0:T(1,128)S(1)} copy-done((s32[1,8]{1,0:T(1,128)S(1)}, s32[1,8]{1,0:T(1,128)}, u32[]{:S(2)}) %copy-start.1) | copy-done | bytes 56
  1.6 28.8 %shard_map.28 = bf16[32,128,256]{2,1,0:T(8,128)(2,1)S(1)} custom-call(s32[1,8]{1,0:T(1,128)S(1)} %copy-done.1, bf16[512,128]{1,0:T(8,128)(2,1)S(1)} %bitcast.3), custom_call_target="tpu_custom_call" | custom-call | tf_op jit(solution)/shard_map/pallas_call | solution.py:249
  30.4 1.3 %copy.4 = bf16[1,1,32,128,256]{4,3,2,1,0:T(8,128)(2,1)} copy(bf16[1,1,32,128,256]{4,3,2,1,0:T(8,128)(2,1)S(1)} %bitcast.2) | data formatting | bytes 4194304
Async XLA Ops:
  0.0 0.9 %copy-start = (bf16[2,32,8,128]{3,2,1,0:T(8,128)(2,1)S(1)}, bf16[2,32,8,128]{3,2,1,0:T(8,128)(2,1)}, u32[]{:S(2)}) copy-start(bf16[2,32,8,128]{3,2,1,0:T(8,128)(2,1)} %param.2) | copy-start | bytes 393220
  0.9 0.7 %copy-start.1 = (s32[1,8]{1,0:T(1,128)S(1)}, s32[1,8]{1,0:T(1,128)}, u32[]{:S(2)}) copy-start(s32[1,8]{1,0:T(1,128)} %tb_hbm.1) | copy-start | bytes 100

commit v3 on v2

--- a/solution.py
+++ b/solution.py
@@ -10,6 +10,7 @@
 LINES = 4
 SHARES = (1, 1, 1, 1)
 CHUNKS = len(SHARES)
+LEAD = 2
 MESH = pl.DeviceIdType.MESH
 
 
@@ -17,7 +18,7 @@
     groups, bands, bins, windows, chunks,
     tb_hbm, x_hbm, out_ref,
     tb_ref, x_ref, raw, power, line_raw, side_raw, line_factor, side_factor, blocks, sums, own, partner,
-    in_sem, p_send, p_recv, line_send, line_recv, first_send, first_recv, side_send, block_recv,
+    in_sem, p_send, p_recv, line_send, relay_send, line_recv, first_send, first_recv, side_send, block_recv,
     lf_send, lf_recv, sf_send, sf_recv, own_send, own_recv, sum_send, sum_recv,
 ):
     g = lax.axis_index("grp")
@@ -74,6 +75,19 @@
     def own_line_copy(t, c):
         return line_copy(row, c, line_send.at[t, c], others[t])
 
+    middle = (row > 0) & (row < LINES - 1)
+
+    def relay_copy(c):
+        return line_copy(others[-1], c, relay_send.at[c], (LINES - 1) * (row - 1))
+
+    def send_line(c):
+        own_line_copy(1, c).start()
+        own_line_copy(0, c).start()
+
+        @pl.when(middle)
+        def _():
+            own_line_copy(2, c).start()
+
     def first_copy(e, c):
         return remote(
             line_raw.at[row, pl.ds(starts[c], sizes[c])], side_raw.at[e, pl.ds(starts[c], sizes[c])],
@@ -117,8 +131,7 @@
         for e in range(len(side)):
             first_copy(e, c).start()
         if c == 0:
-            for t in range(len(others)):
-                own_line_copy(t, c).start()
+            send_line(c)
 
     for e in range(1, bands):
         power_copy(e).wait_recv()
@@ -132,8 +145,7 @@
     for e in range(len(side)):
         side_factor_copy(e).start()
     for c in range(1, chunks):
-        for t in range(len(others)):
-            own_line_copy(t, c).start()
+        send_line(c)
     for f in range(bins):
         v = whiten(line_raw[row, f], factor)
         blocks[g, f] = v
@@ -153,6 +165,11 @@
                 view = line_factor.at[r]
                 remote(view, view, lf_send.at[0], lf_recv.at[r], (g, peer[1])).wait_recv()
             line_copy(r, c, line_send.at[0, c], others[0]).wait_recv()
+            if r is others[-1]:
+                @pl.when(middle)
+                def _():
+                    relay_copy(c).start()
+
             arrive(r, c)
 
     def pick(j, k):
@@ -213,14 +230,15 @@
                 )
                 out_ref[owner * bins + f] = (tile * scale).astype(jnp.bfloat16)
 
-    forward(0)
-    for c in range(chunks):
-        if c + 1 < chunks:
-            forward(c + 1)
-        band_sum(c)
-        if c > 0:
-            gram(c - 1)
-    gram(chunks - 1)
+    for c in range(chunks + LEAD):
+        if c < chunks:
+            forward(c)
+        if c >= LEAD:
+            band_sum(c - LEAD)
+        if c >= chunks:
+            gram(c - chunks)
+    for c in range(LEAD, chunks):
+        gram(c)
 
     for e in range(1, bands):
         power_copy(e).wait_send()
@@ -236,8 +254,13 @@
                 side_copy(e, r, c).wait_send()
         for e in range(1, bands):
             sum_copy(e, c).wait_send()
-        for t in range(len(others)):
+        for t in range(len(others) - 1):
             own_line_copy(t, c).wait_send()
+
+        @pl.when(middle)
+        def _():
+            own_line_copy(2, c).wait_send()
+            relay_copy(c).wait_send()
 
 
 def local(groups, bands, spectra, tile_band):
@@ -268,6 +291,7 @@
             dma((bands - 1,)),
             dma((bands - 1,)),
             dma((LINES - 1, CHUNKS)),
+            dma((CHUNKS,)),
             dma((LINES, CHUNKS)),
             dma((inner - 1, CHUNKS)),
             dma((inner - 1, CHUNKS)),

time: 31.8 us -> 30.9 us (0.972)
  Pallas kernels: 28.8 us -> 27.8 us
    pallas_call x1, Pallas kernels: 28.8 us -> 27.8 us  [local(): pl.pallas_call(functools.partial(kernel, groups, bands, bins, windows, CH...]
where the time goes in v3:
time: 30.9 us; the launch traced here: 30.7 us
  Pallas kernels  27.8 us (90%)
  local copies, waits for them, and re-layouts  2.88 us (9%)
    pallas_call x1, Pallas kernels, local(): pl.pallas_call(functools.partial(kernel, groups, bands, bins, windows, CH...  27.8 us
    unnamed x5, local copies, waits for them, and re-layouts  2.88 us

profile of v3, /device:TPU:0, one launch (start us, length us, event | category | flops | bytes accessed | tf_op | source)
XLA Modules:
  0.0 30.7 jit_solution(4797157458318130686)
XLA Ops:
  0.0 0.0 copy-start
  0.0 0.9 %copy-done = bf16[2,32,8,128]{3,2,1,0:T(8,128)(2,1)S(1)} copy-done((bf16[2,32,8,128]{3,2,1,0:T(8,128)(2,1)S(1)}, bf16[2,32,8,128]{3,2,1,0:T(8,128)(2,1)}, u32[]{:S(2)}) %copy-start) | copy-done | bytes 131096
  0.9 0.0 copy-start.1
  0.9 0.7 %copy-done.1 = s32[1,8]{1,0:T(1,128)S(1)} copy-done((s32[1,8]{1,0:T(1,128)S(1)}, s32[1,8]{1,0:T(1,128)}, u32[]{:S(2)}) %copy-start.1) | copy-done | bytes 56
  1.6 27.8 %shard_map.28 = bf16[32,128,256]{2,1,0:T(8,128)(2,1)S(1)} custom-call(s32[1,8]{1,0:T(1,128)S(1)} %copy-done.1, bf16[512,128]{1,0:T(8,128)(2,1)S(1)} %bitcast.3), custom_call_target="tpu_custom_call" | custom-call | tf_op jit(solution)/shard_map/pallas_call | solution.py:272
  29.4 1.3 %copy.4 = bf16[1,1,32,128,256]{4,3,2,1,0:T(8,128)(2,1)} copy(bf16[1,1,32,128,256]{4,3,2,1,0:T(8,128)(2,1)S(1)} %bitcast.2) | data formatting | bytes 4194304
Async XLA Ops:
  0.0 0.9 %copy-start = (bf16[2,32,8,128]{3,2,1,0:T(8,128)(2,1)S(1)}, bf16[2,32,8,128]{3,2,1,0:T(8,128)(2,1)}, u32[]{:S(2)}) copy-start(bf16[2,32,8,128]{3,2,1,0:T(8,128)(2,1)} %param.2) | copy-start | bytes 393220
  0.9 0.7 %copy-start.1 = (s32[1,8]{1,0:T(1,128)S(1)}, s32[1,8]{1,0:T(1,128)}, u32[]{:S(2)}) copy-start(s32[1,8]{1,0:T(1,128)} %tb_hbm.1) | copy-start | bytes 100
